TPU v7x, 256 devices: a whole 4x4x8 slice. The times are simulated.
256 devices in a mesh: dp: 64 (over z, x, core), tp: 4 (over y).
Axes of the slice: x: 4, y: 4, z: 8, core: 2. Of those that a mesh axis runs over, the one named last changes fastest.
Arguments:
- hidden: bfloat16 [2048, 4096], P('dp', 'tp'), may hold values from -6 to 6
- routes: int32 [2048, 8], P('dp'), may hold values from 0 to 63, all different within a row; in each aligned block of 32 rows (0 to 31, 32 to 63, ...) at most 8 rows name the same one
- routing_weights: float32 [2048, 8], P('dp'), may hold values from 0.05 to 1
- w_gate: bfloat16 [64, 4096, 1536], P('dp', None, 'tp'), may hold values from -0.09375 to 0.09375
- w_up: bfloat16 [64, 4096, 1536], P('dp', None, 'tp'), may hold values from -0.09375 to 0.09375
- w_down: bfloat16 [64, 1536, 4096], P('dp', 'tp'), may hold values from -0.15625 to 0.15625
- norm_gain: float32 [4096], replicated, may hold values from 0.1 to 1.9
- key_projection_weight: bfloat16 [4096, 512], P(None, 'tp'), may hold values from -0.09375 to 0.09375
- value_projection_weight: bfloat16 [4096, 512], P(None, 'tp'), may hold values from -0.09375 to 0.09375
- queries: bfloat16 [2048, 8192], P('dp', 'tp'), may hold values from -128 to 128
- cached_key_rows: bfloat16 [64, 128, 512], P('dp', None, 'tp'), may hold values from -4 to 4
- cached_value_rows: bfloat16 [64, 128, 512], P('dp', None, 'tp'), may hold values from -6 to 6
- lengths: int32 [64], P('dp'), may hold values from 16 to 128
- parents: int32 [64, 32], P('dp'), may hold values from -1 to 30, as said below
Outputs:
- layer_output: bfloat16 [2048, 4096], P('dp', 'tp')
- next_layer_keys: bfloat16 [2048, 512], P('dp', 'tp')
- next_layer_values: bfloat16 [2048, 512], P('dp', 'tp')
- attended: bfloat16 [2048, 8192], P('dp', 'tp')
Inputs may be any that keep to these rules, and one draw needn't show every extreme that they name: `routes`: each row names 8 different experts. In each aligned block of 32 rows (the rows of one device) no expert is named by more than 8 rows, a bound that some block reaches. `parents`: node 0 of each request is the root, with parent -1; every other node i has its parent among nodes max(0, i - 8) to i - 1.
All inputs are finite; a program needn't handle non-finite values.
Results may differ from a plain program's by a relative error of at most 0.013.
Values may be sent and summed in bfloat16 or wider, within the bound.
No kernel may reach another device: no remote copies, remote signals or barrier semaphores. Data moves between devices by JAX's collectives and lax.ppermute only.
A program may use at most 64 MiB of HBM per device.

v0:
```python
import math
import jax
import jax.numpy as jnp
from jax import lax
from jax.sharding import PartitionSpec as P

HEAD_SIZE = 128


def split_up(shard, dim, size):
    shape = shard.shape
    tiles = shard.reshape(*shape[:dim], size, shape[dim] // size, *shape[dim + 1 :])
    return jnp.moveaxis(tiles, dim, 0)


def sent_and_summed(shard, axis, dim):
    size = lax.axis_size(axis)
    tiles = lax.all_to_all(split_up(shard, dim, size), axis, 0, 0, tiled=True)
    return jnp.sum(tiles.astype(jnp.float32), axis=0)


def joined_along(tiles, dim):
    shape = list(tiles.shape[1:])
    shape[dim] *= tiles.shape[0]
    return jnp.moveaxis(tiles, 0, dim).reshape(shape)


def copy_for_each(shard, axis):
    copies = jnp.broadcast_to(shard, (lax.axis_size(axis), *shard.shape))
    return lax.all_to_all(copies, axis, split_axis=0, concat_axis=0, tiled=True)


def gathered_copies(shard, axis, dim):
    return joined_along(copy_for_each(shard, axis), dim)


def ancestry(parent_row):
    node_count = parent_row.shape[0]
    position = jnp.arange(node_count, dtype=jnp.int32)
    reached = (parent_row[:, None] == position[None, :]).astype(jnp.float32)
    reached = reached + jnp.eye(node_count, dtype=jnp.float32)
    for doubling in range((node_count - 1).bit_length()):
        reached = jnp.minimum(jnp.dot(reached, reached, preferred_element_type=jnp.float32), 1.0)
    return reached > 0.5


def quarter_to_whole(received):
    return lax.all_gather(received, "tp", axis=2, tiled=True)


def attend_local(
    queries, cached_key_rows, cached_value_rows, tree_key_rows, tree_value_rows, lengths, parents
):
    request_count = lengths.shape[0]
    node_count = parents.shape[1]
    slot_length = cached_key_rows.shape[1]
    kv_local = cached_key_rows.shape[2] // HEAD_SIZE
    query_group_count = queries.shape[1] // (kv_local * HEAD_SIZE)
    scaled = 1.0 / math.sqrt(HEAD_SIZE)
    tree_query_block = queries.reshape(
        request_count, node_count, kv_local, query_group_count, HEAD_SIZE
    )
    joined_key_block = cached_key_rows.reshape(request_count, slot_length, kv_local, HEAD_SIZE)
    joined_value_block = cached_value_rows.reshape(request_count, slot_length, kv_local, HEAD_SIZE)
    tree_key_block = tree_key_rows.reshape(request_count, node_count, kv_local, HEAD_SIZE)
    tree_value_block = tree_value_rows.reshape(request_count, node_count, kv_local, HEAD_SIZE)
    cache_scores = (
        jnp.einsum(
            "rnkgd,rpkd->rkgnp",
            tree_query_block,
            joined_key_block,
            preferred_element_type=jnp.float32,
        )
        * scaled
    )
    tree_scores = (
        jnp.einsum(
            "rnkgd,rmkd->rkgnm",
            tree_query_block,
            tree_key_block,
            preferred_element_type=jnp.float32,
        )
        * scaled
    )
    visible = jnp.arange(slot_length, dtype=jnp.int32)[None, :] < lengths[:, None]
    cache_scores = jnp.where(visible[:, None, None, None, :], cache_scores, -1e30)
    related = jax.vmap(ancestry)(parents)
    tree_scores = jnp.where(related[:, None, None], tree_scores, -1e30)
    highest = jnp.maximum(jnp.max(cache_scores, axis=-1), jnp.max(tree_scores, axis=-1))[..., None]
    cache_raised = jnp.exp(cache_scores - highest)
    tree_raised = jnp.exp(tree_scores - highest)
    denominator = jnp.sum(cache_raised, axis=-1, keepdims=True) + jnp.sum(
        tree_raised, axis=-1, keepdims=True
    )
    cache_weights = (cache_raised / denominator).astype(jnp.bfloat16)
    tree_weights = (tree_raised / denominator).astype(jnp.bfloat16)
    output = jnp.einsum(
        "rkgnp,rpkd->rnkgd", cache_weights, joined_value_block, preferred_element_type=jnp.float32
    )
    output = output + jnp.einsum(
        "rkgnm,rmkd->rnkgd", tree_weights, tree_value_block, preferred_element_type=jnp.float32
    )
    return output.reshape(request_count * node_count, -1).astype(jnp.bfloat16)


def on_device(
    hidden,
    routes,
    routing_weights,
    w_gate,
    w_up,
    w_down,
    norm_gain,
    key_projection_weight,
    value_projection_weight,
    queries,
    cached_key_rows,
    cached_value_rows,
    lengths,
    parents,
):
    token_count = hidden.shape[0]
    top_count = routes.shape[1]
    local_experts = w_gate.shape[0]
    expert_count = lax.axis_size("dp") * local_experts
    capacity = min(token_count, 2 * token_count * top_count // expert_count)
    column_count = hidden.shape[1]
    weights = routing_weights / jnp.sum(routing_weights, axis=1, keepdims=True)
    expert_ids = jnp.arange(expert_count, dtype=jnp.int32)
    chosen = routes[:, :, None] == expert_ids[None, None, :]
    member = jnp.any(chosen, axis=1)
    portion = jnp.sum(jnp.where(chosen, weights[:, :, None], 0.0), axis=1)
    earlier = jnp.tril(jnp.ones((token_count, token_count), jnp.bfloat16), -1)
    rank = jnp.dot(earlier, member.astype(jnp.bfloat16), preferred_element_type=jnp.float32)
    slots = jnp.arange(capacity, dtype=jnp.float32)
    placed = member.T[:, None, :] & (rank.T[:, None, :] == slots[None, :, None])
    placed = placed.reshape(expert_count * capacity, token_count)
    outgoing = jnp.dot(
        placed.astype(jnp.bfloat16), hidden, preferred_element_type=jnp.float32
    ).astype(jnp.bfloat16)
    outgoing = outgoing.reshape(expert_count, capacity, column_count)
    received = quarter_to_whole(
        lax.all_to_all(outgoing, "dp", split_axis=0, concat_axis=0, tiled=True)
    )
    slot_count = received.shape[1]
    grouped = received.reshape(-1, local_experts, slot_count, received.shape[2])
    gate_act = jnp.einsum("secd,edf->secf", grouped, w_gate, preferred_element_type=jnp.float32)
    upward = jnp.einsum("secd,edf->secf", grouped, w_up, preferred_element_type=jnp.float32)
    active = (jax.nn.silu(gate_act) * upward).astype(jnp.bfloat16)
    partial_value = jnp.einsum("secf,efd->secd", active, w_down, preferred_element_type=jnp.float32)
    partial_value = partial_value.reshape(received.shape[0], slot_count, partial_value.shape[3])
    summed = sent_and_summed(partial_value.astype(jnp.bfloat16), "tp", 2)
    back = lax.all_to_all(
        summed.astype(jnp.bfloat16), "dp", split_axis=0, concat_axis=0, tiled=True
    )
    flat_back = back.reshape(expert_count * capacity, back.shape[2])
    spread = jnp.broadcast_to(portion.T[:, None, :], (expert_count, capacity, token_count))
    spread = jnp.where(placed, spread.reshape(expert_count * capacity, token_count), 0.0)
    upper = spread.astype(jnp.bfloat16)
    lower = (spread - upper.astype(jnp.float32)).astype(jnp.bfloat16)
    both = jnp.concatenate([upper, lower], axis=1)
    mixed = lax.dot_general(
        both, flat_back, (((0,), (0,)), ((), ())), preferred_element_type=jnp.float32
    )
    expert_mix = mixed[:token_count] + mixed[token_count:]
    own_out = (hidden.astype(jnp.float32) + expert_mix).astype(jnp.bfloat16)
    full_out = gathered_copies(own_out, "tp", 1)
    widened = full_out.astype(jnp.float32)
    scaling = lax.rsqrt(jnp.mean(widened * widened, axis=1, keepdims=True) + 1e-06)
    normed = (widened * scaling * norm_gain).astype(jnp.bfloat16)
    tree_key_rows = jnp.dot(
        normed, key_projection_weight, preferred_element_type=jnp.float32
    ).astype(jnp.bfloat16)
    tree_value_rows = jnp.dot(
        normed, value_projection_weight, preferred_element_type=jnp.float32
    ).astype(jnp.bfloat16)
    attended = attend_local(
        queries,
        cached_key_rows,
        cached_value_rows,
        tree_key_rows,
        tree_value_rows,
        lengths,
        parents,
    )
    return (own_out, tree_key_rows, tree_value_rows, attended)


def solution(mesh):
    return jax.shard_map(
        on_device,
        mesh=mesh,
        in_specs=(
            P("dp", "tp"),
            P("dp", None),
            P("dp", None),
            P("dp", None, "tp"),
            P("dp", None, "tp"),
            P("dp", "tp", None),
            P(),
            P(None, "tp"),
            P(None, "tp"),
            P("dp", "tp"),
            P("dp", None, "tp"),
            P("dp", None, "tp"),
            P("dp"),
            P("dp", None),
        ),
        out_specs=(P("dp", "tp"), P("dp", "tp"), P("dp", "tp"), P("dp", "tp")),
        check_vma=False,
    )
```

profile of v0, /device:TPU:2, one launch (start us, length us, event | category | flops | bytes accessed | tf_op | source)
XLA Modules:
  0.0 239.4 jit_solution(4586139410621288270)
XLA Ops:
  7.2 0.9 copy.67
  8.2 0.7 reduce_sum.57
  8.9 0.7 broadcast_divide_fusion
  10.9 1.3 fusion.5
  12.2 40.7 %all_to_all.20 = bf16[64,8,1024]{2,1,0:T(8,128)(2,1)} all-to-all(bf16[64,8,1024]{2,1,0:T(8,128)(2,1)S(1)} %fusion.5), channel_id=1, replica_groups=mesh['dp'=64,'tp'=4] {'dp'}, dimensions={0} | all-to-all | bytes 2097152 | tf_op jit(solution)/shard_map/all_to_all | solution.py:143
  52.9 47.6 %all-gather.2.cloned.1.call-done = bf16[64,8,4096]{2,1,0:T(8,128)(2,1)} async-done(((bf16[64,8,1024]{2,1,0:T(8,128)(2,1)}), bf16[64,8,4096]{2,1,0:T(8,128)(2,1)}) %all-gather.2.cloned.1.call-update) | async-done | bytes 4194320 | tf_op jit(solution)/shard_map/all_gather | solution.py:48
  100.5 6.4 %fusion.6 = f32[64,1,8,384]{3,2,0,1:T(8,128)} fusion(bf16[64,8,4096]{2,1,0:T(8,128)(2,1)} %all-gather.2.cloned.1.call-done, bf16[1,4096,384]{2,1,0:T(8,128)(2,1)} %param.17), kind=kOutput, calls=%fused_computation.9 | convolution fusion | flops 1610612736 | bytes 8126464 | tf_op jit(solution)/shard_map/secd,edf->secf/dot_general | solution.py:147
  107.0 9.7 %convolution_convert_fusion = bf16[64,8,4096]{2,1,0:T(8,128)(2,1)} fusion(bf16[1,384,4096]{2,1,0:T(8,128)(2,1)S(1)} %copy-done, bf16[64,8,4096]{2,1,0:T(8,128)(2,1)} %all-gather.2.cloned.1.call-done, bf16[1,4096,384]{2,1,0:T(8,128)(2,1)} %param.18, f32[64,1,8,384]{3,2,0,1:T(8,128)} %fusion.6), kind=kOutput, calls=%fused_computation | convolution fusion | flops 3224502272 | bytes 15466496 | tf_op jit(solution)/shard_map/secf,efd->secd/dot_general | solution.py:150
  116.7 2.6 %copy.101 = bf16[64,8,4,1024]{3,1,0,2:T(8,128)(2,1)S(1)} copy(bf16[64,8,4,1024]{3,1,2,0:T(8,128)(2,1)} %bitcast.160) | data formatting | bytes 8388608 | tf_op jit(solution)/shard_map/convert_element_type | solution.py:152
  119.3 52.5 %all_to_all.21 = bf16[4,64,8,1024]{3,2,1,0:T(8,128)(2,1)} all-to-all(bf16[4,64,8,1024]{3,2,1,0:T(8,128)(2,1)S(1)} %bitcast.157), channel_id=1, replica_groups=mesh['dp'=64,'tp'=4] {'tp'}, dimensions={0} | all-to-all | bytes 8388608 | tf_op jit(solution)/shard_map/all_to_all | solution.py:18
  171.8 4.4 %reduce_sum.59 = bf16[64,8,1024]{2,1,0:T(8,128)(2,1)} reduce(bf16[4,64,8,1024]{3,2,1,0:T(8,128)(2,1)} %all_to_all.21, bf16[]{:T(256)} %constant.15.clone.1), dimensions={0}, to_apply=%region_3.4 | reduce | flops 1572864 | bytes 5242882 | tf_op jit(solution)/shard_map/reduce_sum | solution.py:19
  176.2 10.8 %all-to-all-start.2 = ((bf16[64,8,1024]{2,1,0:T(8,128)(2,1)}), bf16[64,8,1024]{2,1,0:T(8,128)(2,1)}, u32[]{:S(2)}, u32[]{:S(2)}) async-start(bf16[64,8,1024]{2,1,0:T(8,128)(2,1)} %reduce_sum.59), calls=%async_computation.2 | async-start | bytes 2097152 | tf_op jit(solution)/shard_map/all_to_all | solution.py:153
  187.8 0.7 copy.78
  189.1 0.5 iota_compare_fusion.2
  189.7 26.1 %all-to-all-done.2 = bf16[64,8,1024]{2,1,0:T(8,128)(2,1)} async-done(((bf16[64,8,1024]{2,1,0:T(8,128)(2,1)}), bf16[64,8,1024]{2,1,0:T(8,128)(2,1)}, u32[]{:S(2)}, u32[]{:S(2)}) %all-to-all-start.2) | async-done | bytes 1048608 | tf_op jit(solution)/shard_map/all_to_all | solution.py:153
  215.8 1.6 fusion.29
  217.4 0.7 broadcast_in_dim.81
  218.1 3.4 %all-to-all-start.3 = ((bf16[4,32,1024]{2,1,0:T(8,128)(2,1)}), bf16[4,32,1024]{2,1,0:T(8,128)(2,1)S(1)}, u32[]{:S(2)}, u32[]{:S(2)}) async-start(bf16[4,32,1024]{2,1,0:T(8,128)(2,1)} %broadcast_in_dim.81), calls=%async_computation.3 | async-start | bytes 524288 | tf_op jit(solution)/shard_map/all_to_all | solution.py:30
  221.5 2.4 %fusion.71 = (f32[16,32]{1,0:T(8,128)}, f32[1,1,16,32,128]{4,3,2,1,0:T(8,128)}) fusion(bf16[1,128,128]{2,1,0:T(8,128)(2,1)} %param.24, pred[128]{0:T(512)(128)(4,1)} %iota_compare_fusion.2, bf16[32,2048]{1,0:T(8,128)(2,1)} %param.23), kind=kOutput, calls=%fused_computation.96 | convolution fusion | flops 16973312 | bytes 428160 | tf_op jit(solution)/shard_map/rnkgd,rpkd->rkgnp/dot_general | solution.py:68
  223.9 4.2 %all-to-all-done.3 = bf16[4,32,1024]{2,1,0:T(8,128)(2,1)S(1)} async-done(((bf16[4,32,1024]{2,1,0:T(8,128)(2,1)}), bf16[4,32,1024]{2,1,0:T(8,128)(2,1)S(1)}, u32[]{:S(2)}, u32[]{:S(2)}) %all-to-all-start.3) | async-done | bytes 262176 | tf_op jit(solution)/shard_map/all_to_all | solution.py:30
  228.5 1.7 convolution_convert_fusion.3
  230.9 0.3 convolution_convert_fusion.2
  231.3 0.3 convolution_bitcast_fusion
  231.9 0.7 copy.102
  (61 shorter events, 3.4 us)
Async XLA Ops:
  7.2 99.8 %copy-start = (bf16[1,384,4096]{2,1,0:T(8,128)(2,1)S(1)}, bf16[1,384,4096]{2,1,0:T(8,128)(2,1)}, u32[]{:S(2)}) copy-start(bf16[1,384,4096]{2,1,0:T(8,128)(2,1)} %param.19) | copy-start | bytes 9437188
  7.2 93.3 %all-gather.2.cloned.1.call-start = ((), (), s32[]{:S(2)}) async-start(), calls=%async_computation.4 | async-start | bytes 5242880 | tf_op jit(solution)/shard_map/all_gather | solution.py:48
  171.8 15.3 %copy-start.11 = (s32[1,32]{1,0:T(1,128)S(1)}, s32[1,32]{1,0:T(1,128)}, u32[]{:S(2)}) copy-start(s32[1,32]{1,0:T(1,128)} %param.27) | copy-start | bytes 388
  176.2 41.1 %copy-start.4 = (bf16[32,1024]{1,0:T(8,128)(2,1)S(1)}, bf16[32,1024]{1,0:T(8,128)(2,1)}, u32[]{:S(2)}) copy-start(bf16[32,1024]{1,0:T(8,128)(2,1)} %param.14) | copy-start | bytes 196612
  176.2 39.6 %all-to-all-start.2 = ((bf16[64,8,1024]{2,1,0:T(8,128)(2,1)}), bf16[64,8,1024]{2,1,0:T(8,128)(2,1)}, u32[]{:S(2)}, u32[]{:S(2)}) async-start(bf16[64,8,1024]{2,1,0:T(8,128)(2,1)} %reduce_sum.59), calls=%async_computation.2 | async-start | bytes 2097152 | tf_op jit(solution)/shard_map/all_to_all | solution.py:153
  187.0 41.4 %copy-start.6 = (f32[4096]{0:T(1024)S(1)}, f32[4096]{0:T(1024)}, u32[]{:S(2)}) copy-start(f32[4096]{0:T(1024)} %param.20) | copy-start | bytes 49156
  215.8 14.4 %copy-start.3 = (bf16[32,2048]{1,0:T(8,128)(2,1)S(1)}, bf16[32,2048]{1,0:T(8,128)(2,1)}, u32[]{:S(2)}) copy-start(bf16[32,2048]{1,0:T(8,128)(2,1)} %param.23) | copy-start | bytes 393220
  217.4 0.7 copy-start.5
  218.1 10.1 %all-to-all-start.3 = ((bf16[4,32,1024]{2,1,0:T(8,128)(2,1)}), bf16[4,32,1024]{2,1,0:T(8,128)(2,1)S(1)}, u32[]{:S(2)}, u32[]{:S(2)}) async-start(bf16[4,32,1024]{2,1,0:T(8,128)(2,1)} %broadcast_in_dim.81), calls=%async_computation.3 | async-start | bytes 524288 | tf_op jit(solution)/shard_map/all_to_all | solution.py:30
  228.2 2.0 copy-start.9
  228.2 2.4 copy-start.8
  228.2 2.5 %copy-start.2 = (f32[1,1,16,32,128]{4,3,2,1,0:T(8,128)S(1)}, f32[1,1,16,32,128]{4,3,2,1,0:T(8,128)}, u32[]{:S(2)}) copy-start(f32[1,1,16,32,128]{4,3,2,1,0:T(8,128)} %get-tuple-element.7) | copy-start | bytes 786436
  228.2 2.7 %copy-start.1 = (bf16[4096,128]{1,0:T(8,128)(2,1)S(1)}, bf16[4096,128]{1,0:T(8,128)(2,1)}, u32[]{:S(2)}) copy-start(bf16[4096,128]{1,0:T(8,128)(2,1)} %param.22) | copy-start | bytes 3145732
  228.2 3.1 %copy-start.12 = (bf16[1,128,128]{2,1,0:T(8,128)(2,1)S(1)}, bf16[1,128,128]{2,1,0:T(8,128)(2,1)}, u32[]{:S(2)}) copy-start(bf16[1,128,128]{2,1,0:T(8,128)(2,1)} %param.25) | copy-start | bytes 98308
  230.2 2.4 %copy-start.7 = (bf16[32,128]{1,0:T(8,128)(2,1)}, bf16[32,128]{1,0:T(8,128)(2,1)S(1)}, u32[]{:S(2)}) copy-start(bf16[32,128]{1,0:T(8,128)(2,1)S(1)} %convolution_convert_fusion.3) | copy-start | bytes 24580
  231.2 1.4 copy-start.10
Sparse Core Ops, SparseCore 0:
  53.0 47.4 all-gather.1
where the time goes:
time: 240 us; the launch traced here: 239 us
  blocking collectives  93.2 us (39%)
  waiting for transfers between devices  77.9 us (32%)
  matrix products  25.2 us (10%)
  between operations  15 us (6%)
  starting transfers between devices  14.3 us (6%)
  other arithmetic  7.3 us (3%)
  local copies, waits for them, and re-layouts  6.57 us (3%)
    all_to_all x1, blocking collectives, sent_and_summed(): tiles = lax.all_to_all(split_up(shard, dim, size), axis, 0, 0, tiled=True)  52.5 us
    all_gather x1, waiting for transfers between devices, quarter_to_whole(): return lax.all_gather(received, 'tp', axis=2, tiled=True)  47.6 us
    all_to_all x1, blocking collectives, on_device(): lax.all_to_all(outgoing, 'dp', split_axis=0, concat_axis=0, tiled=True)  40.7 us
    all_to_all x1, waiting for transfers between devices, on_device(): lax.all_to_all(summed.astype(jnp.bfloat16), 'dp', split_axis=0, concat_ax...  26.1 us
    all_to_all x1, starting transfers between devices, on_device(): lax.all_to_all(summed.astype(jnp.bfloat16), 'dp', split_axis=0, concat_ax...  10.8 us
    dot_general x1, matrix products, on_device(): jnp.einsum('secf,efd->secd', active, w_down, preferred_element_type=jnp.f...  9.74 us
    dot_general x1, matrix products, on_device(): jnp.einsum('secd,edf->secf', grouped, w_gate, preferred_element_type=jnp....  6.43 us
  transfers between devices with their start and end apart: 3, of which 3 were waited for; matrix products, arithmetic and copies ran while one was open for 2% of the time, Pallas kernels for 0%

commit v1 on v0

--- a/solution.py
+++ b/solution.py
@@ -5,6 +5,14 @@
 from jax.sharding import PartitionSpec as P
 
 HEAD_SIZE = 128
+
+
+def tiled_gather(shard, axis, dim):
+    size = lax.axis_size(axis)
+    repeats = [size if d == dim else 1 for d in range(shard.ndim)]
+    return lax.all_to_all(
+        jnp.tile(shard, repeats), axis, split_axis=dim, concat_axis=dim, tiled=True
+    )
 
 
 def split_up(shard, dim, size):
@@ -45,7 +53,7 @@
 
 
 def quarter_to_whole(received):
-    return lax.all_gather(received, "tp", axis=2, tiled=True)
+    return tiled_gather(received, "tp", 2)
 
 
 def attend_local(

time: 240 us -> 271 us (1.13)
  blocking collectives: 93.2 us -> 145 us
  waiting for transfers between devices: 77.9 us -> 32 us
  local copies, waits for them, and re-layouts: 6.57 us -> 46.8 us
  between operations: 15 us -> 1.59 us
    all_to_all x0 -> x1, blocking collectives: none -> 53.9 us  [tiled_gather(): lax.all_to_all(jnp.tile(shard, repeats), axis, split_axis=dim, concat_axi...]
    all_gather x1 -> x0, waiting for transfers between devices: 47.6 us -> none  [quarter_to_whole(): return lax.all_gather(received, 'tp', axis=2, tiled=True)]
    unnamed x28 -> x26, local copies, waits for them, and re-layouts: 1.67 us -> 20.4 us
    all_to_all x0 -> x2, local copies, waits for them, and re-layouts: none -> 16.2 us  [the longest x1 12 us: tiled_gather(): lax.all_to_all(jnp.tile(shard, repeats), axis, split_axis=dim, concat_axi...]
    another operation x0 -> x1, local copies, waits for them, and re-layouts: none -> 5.89 us  [tiled_gather(): jnp.tile(shard, repeats)]
  transfers between devices with their start and end apart: 3 -> 2, of which waited for: 3 -> 2; matrix products, arithmetic and copies ran while one was open for 2% -> 1% of each run, Pallas kernels for 0% -> 0%
where the time goes in v1:
time: 271 us; the launch traced here: 270 us
  blocking collectives  145 us (54%)
  local copies, waits for them, and re-layouts  46.8 us (17%)
  waiting for transfers between devices  32 us (12%)
  matrix products  25.4 us (9%)
  starting transfers between devices  11.6 us (4%)
  other arithmetic  6.83 us (3%)
    all_to_all x1, blocking collectives, tiled_gather(): lax.all_to_all(jnp.tile(shard, repeats), axis, split_axis=dim, concat_axi...  53.9 us
    all_to_all x1, blocking collectives, sent_and_summed(): tiles = lax.all_to_all(split_up(shard, dim, size), axis, 0, 0, tiled=True)  50.7 us
    all_to_all x1, blocking collectives, on_device(): lax.all_to_all(outgoing, 'dp', split_axis=0, concat_axis=0, tiled=True)  40.7 us
    all_to_all x1, waiting for transfers between devices, on_device(): lax.all_to_all(summed.astype(jnp.bfloat16), 'dp', split_axis=0, concat_ax...  27.2 us
    unnamed x26, local copies, waits for them, and re-layouts  20.4 us
    all_to_all x1, local copies, waits for them, and re-layouts, tiled_gather(): lax.all_to_all(jnp.tile(shard, repeats), axis, split_axis=dim, concat_axi...  12 us
    dot_general x1, matrix products, on_device(): jnp.einsum('secf,efd->secd', active, w_down, preferred_element_type=jnp.f...  9.73 us
    all_to_all x1, starting transfers between devices, on_device(): lax.all_to_all(summed.astype(jnp.bfloat16), 'dp', split_axis=0, concat_ax...  8.2 us
  transfers between devices with their start and end apart: 2, of which 2 were waited for; matrix products, arithmetic and copies ran while one was open for 1% of the time, Pallas kernels for 0%

profile of v1, /device:TPU:2, one launch (start us, length us, event | category | flops | bytes accessed | tf_op | source)
XLA Modules:
  0.0 269.6 jit_solution(13264621185390337528)
XLA Ops:
  0.7 0.9 copy.90
  1.6 0.7 reduce_sum.57
  4.3 1.3 fusion.5
  5.6 40.7 %all_to_all.25 = bf16[64,8,1024]{2,1,0:T(8,128)(2,1)} all-to-all(bf16[64,8,1024]{2,1,0:T(8,128)(2,1)S(1)} %fusion.5), channel_id=1, replica_groups=mesh['dp'=64,'tp'=4] {'dp'}, dimensions={0} | all-to-all | bytes 2097152 | tf_op jit(solution)/shard_map/all_to_all | solution.py:151
  46.3 4.2 %copy.98 = bf16[64,8,1024]{0,1,2:T(8,128)(2,1)} copy(bf16[64,8,1024]{2,1,0:T(8,128)(2,1)} %all_to_all.25) | data formatting | bytes 2097152 | tf_op jit(solution)/shard_map/all_to_all | solution.py:151
  50.5 5.9 %tile.4 = bf16[64,8,4,1024]{0,1,3,2:T(8,128)(2,1)} broadcast(bf16[64,8,1024]{0,1,2:T(8,128)(2,1)} %copy.98), dimensions={0,1,3} | broadcast | bytes 5242880 | tf_op jit(solution)/shard_map/tile | solution.py:14
  56.4 9.5 %reshape.325 = bf16[4,2,262144]{2,1,0:T(2,128)(2,1)} reshape(bf16[4096,8,64]{2,1,0:T(8,128)(2,1)} %bitcast.160) | data formatting | bytes 8388608
  65.9 53.9 %all_to_all.26 = bf16[4,2,262144]{2,1,0:T(2,128)(2,1)} all-to-all(bf16[4,2,262144]{2,1,0:T(2,128)(2,1)} %reshape.325), channel_id=1, replica_groups=mesh['dp'=64,'tp'=4] {'tp'}, dimensions={0} | all-to-all | bytes 8388608 | tf_op jit(solution)/shard_map/all_to_all | solution.py:13
  119.8 9.2 %reshape.326 = bf16[4096,8,64]{2,1,0:T(8,128)(2,1)} reshape(bf16[4,2,262144]{2,1,0:T(2,128)(2,1)} %all_to_all.26) | data formatting | bytes 8388608
  129.1 12.0 %copy.99 = bf16[64,8,4096]{2,1,0:T(8,128)(2,1)} copy(bf16[64,8,4096]{0,1,2:T(8,128)(2,1)} %bitcast.161) | data formatting | bytes 8388608 | tf_op jit(solution)/shard_map/all_to_all | solution.py:13
  141.1 6.4 %fusion.6 = f32[64,1,8,384]{3,2,0,1:T(8,128)} fusion(bf16[64,8,4096]{2,1,0:T(8,128)(2,1)} %copy.99, bf16[1,4096,384]{2,1,0:T(8,128)(2,1)} %param.17), kind=kOutput, calls=%fused_computation.9 | convolution fusion | flops 1610612736 | bytes 8126464 | tf_op jit(solution)/shard_map/secd,edf->secf/dot_general | solution.py:155
  147.5 9.7 %convolution_convert_fusion = bf16[64,8,4096]{2,1,0:T(8,128)(2,1)} fusion(bf16[1,384,4096]{2,1,0:T(8,128)(2,1)S(1)} %copy-done, bf16[64,8,4096]{2,1,0:T(8,128)(2,1)} %copy.99, bf16[1,4096,384]{2,1,0:T(8,128)(2,1)} %param.18, f32[64,1,8,384]{3,2,0,1:T(8,128)} %fusion.6), kind=kOutput, calls=%fused_computation | convolution fusion | flops 3224502272 | bytes 15466496 | tf_op jit(solution)/shard_map/secf,efd->secd/dot_general | solution.py:158
  157.2 2.6 copy.127
  159.9 50.7 %all_to_all.27 = bf16[4,64,8,1024]{3,2,1,0:T(8,128)(2,1)} all-to-all(bf16[4,64,8,1024]{3,2,1,0:T(8,128)(2,1)S(1)} %bitcast.162), channel_id=1, replica_groups=mesh['dp'=64,'tp'=4] {'tp'}, dimensions={0} | all-to-all | bytes 8388608 | tf_op jit(solution)/shard_map/all_to_all | solution.py:26
  210.6 4.4 %reduce_sum.59 = bf16[64,8,1024]{2,1,0:T(8,128)(2,1)} reduce(bf16[4,64,8,1024]{3,2,1,0:T(8,128)(2,1)} %all_to_all.27, bf16[]{:T(256)} %constant.15.clone.1), dimensions={0}, to_apply=%region_3.4 | reduce | flops 1572864 | bytes 5242882 | tf_op jit(solution)/shard_map/reduce_sum | solution.py:27
  215.0 8.2 %all-to-all-start.3 = ((bf16[64,8,1024]{2,1,0:T(8,128)(2,1)}), bf16[64,8,1024]{2,1,0:T(8,128)(2,1)}, u32[]{:S(2)}, u32[]{:S(2)}) async-start(bf16[64,8,1024]{2,1,0:T(8,128)(2,1)} %reduce_sum.59), calls=%async_computation.3 | async-start | bytes 2097152 | tf_op jit(solution)/shard_map/all_to_all | solution.py:161
  224.7 27.2 %all-to-all-done.3 = bf16[64,8,1024]{2,1,0:T(8,128)(2,1)} async-done(((bf16[64,8,1024]{2,1,0:T(8,128)(2,1)}), bf16[64,8,1024]{2,1,0:T(8,128)(2,1)}, u32[]{:S(2)}, u32[]{:S(2)}) %all-to-all-start.3) | async-done | bytes 1048608 | tf_op jit(solution)/shard_map/all_to_all | solution.py:161
  251.9 1.5 fusion.29
  253.5 0.7 broadcast_in_dim.81
  254.2 3.4 %all-to-all-start.4 = ((bf16[4,32,1024]{2,1,0:T(8,128)(2,1)}), bf16[4,32,1024]{2,1,0:T(8,128)(2,1)S(1)}, u32[]{:S(2)}, u32[]{:S(2)}) async-start(bf16[4,32,1024]{2,1,0:T(8,128)(2,1)} %broadcast_in_dim.81), calls=%async_computation.4 | async-start | bytes 524288 | tf_op jit(solution)/shard_map/all_to_all | solution.py:38
  257.6 1.8 fusion.71
  259.4 4.8 %all-to-all-done.4 = bf16[4,32,1024]{2,1,0:T(8,128)(2,1)S(1)} async-done(((bf16[4,32,1024]{2,1,0:T(8,128)(2,1)}), bf16[4,32,1024]{2,1,0:T(8,128)(2,1)S(1)}, u32[]{:S(2)}, u32[]{:S(2)}) %all-to-all-start.4) | async-done | bytes 262176 | tf_op jit(solution)/shard_map/all_to_all | solution.py:38
  264.5 1.7 convolution_convert_fusion.3
  266.2 1.2 fusion.72
  (60 shorter events, 5.1 us)
Async XLA Ops:
  0.6 146.9 %copy-start = (bf16[1,384,4096]{2,1,0:T(8,128)(2,1)S(1)}, bf16[1,384,4096]{2,1,0:T(8,128)(2,1)}, u32[]{:S(2)}) copy-start(bf16[1,384,4096]{2,1,0:T(8,128)(2,1)} %param.19) | copy-start | bytes 9437188
  210.6 12.6 %copy-start.9 = (s32[1,32]{1,0:T(1,128)S(1)}, s32[1,32]{1,0:T(1,128)}, u32[]{:S(2)}) copy-start(s32[1,32]{1,0:T(1,128)} %param.27) | copy-start | bytes 388
  210.6 42.9 %copy-start.3 = (bf16[32,1024]{1,0:T(8,128)(2,1)S(1)}, bf16[32,1024]{1,0:T(8,128)(2,1)}, u32[]{:S(2)}) copy-start(bf16[32,1024]{1,0:T(8,128)(2,1)} %param.14) | copy-start | bytes 196612
  210.6 47.0 %copy-start.7 = (bf16[1,128,128]{2,1,0:T(8,128)(2,1)S(1)}, bf16[1,128,128]{2,1,0:T(8,128)(2,1)}, u32[]{:S(2)}) copy-start(bf16[1,128,128]{2,1,0:T(8,128)(2,1)} %param.24) | copy-start | bytes 98308
  215.0 49.6 %copy-start.5 = (f32[4096]{0:T(1024)S(1)}, f32[4096]{0:T(1024)}, u32[]{:S(2)}) copy-start(f32[4096]{0:T(1024)} %param.20) | copy-start | bytes 49156
  215.0 36.9 %all-to-all-start.3 = ((bf16[64,8,1024]{2,1,0:T(8,128)(2,1)}), bf16[64,8,1024]{2,1,0:T(8,128)(2,1)}, u32[]{:S(2)}, u32[]{:S(2)}) async-start(bf16[64,8,1024]{2,1,0:T(8,128)(2,1)} %reduce_sum.59), calls=%async_computation.3 | async-start | bytes 2097152 | tf_op jit(solution)/shard_map/all_to_all | solution.py:161
  253.5 15.1 %copy-start.4 = (bf16[32,1024]{1,0:T(8,128)(2,1)}, bf16[32,1024]{1,0:T(8,128)(2,1)S(1)}, u32[]{:S(2)}) copy-start(bf16[32,1024]{1,0:T(8,128)(2,1)S(1)} %fusion.40) | copy-start | bytes 196612
  254.2 10.1 %all-to-all-start.4 = ((bf16[4,32,1024]{2,1,0:T(8,128)(2,1)}), bf16[4,32,1024]{2,1,0:T(8,128)(2,1)S(1)}, u32[]{:S(2)}, u32[]{:S(2)}) async-start(bf16[4,32,1024]{2,1,0:T(8,128)(2,1)} %broadcast_in_dim.81), calls=%async_computation.4 | async-start | bytes 524288 | tf_op jit(solution)/shard_map/all_to_all | solution.py:38
  264.3 3.3 %copy-start.2 = (f32[1,1,16,32,128]{4,3,2,1,0:T(8,128)S(1)}, f32[1,1,16,32,128]{4,3,2,1,0:T(8,128)}, u32[]{:S(2)}) copy-start(f32[1,1,16,32,128]{4,3,2,1,0:T(8,128)} %get-tuple-element.7) | copy-start | bytes 786436
  264.3 3.6 %copy-start.1 = (bf16[4096,128]{1,0:T(8,128)(2,1)S(1)}, bf16[4096,128]{1,0:T(8,128)(2,1)}, u32[]{:S(2)}) copy-start(bf16[4096,128]{1,0:T(8,128)(2,1)} %param.22) | copy-start | bytes 3145732
  264.3 3.9 %copy-start.10 = (bf16[1,128,128]{2,1,0:T(8,128)(2,1)S(1)}, bf16[1,128,128]{2,1,0:T(8,128)(2,1)}, u32[]{:S(2)}) copy-start(bf16[1,128,128]{2,1,0:T(8,128)(2,1)} %param.25) | copy-start | bytes 98308
  266.2 3.3 %copy-start.6 = (bf16[32,128]{1,0:T(8,128)(2,1)}, bf16[32,128]{1,0:T(8,128)(2,1)S(1)}, u32[]{:S(2)}) copy-start(bf16[32,128]{1,0:T(8,128)(2,1)S(1)} %convolution_convert_fusion.3) | copy-start | bytes 24580
  268.2 1.4 copy-start.8
